TPU v7x, 256 devices: a whole 4x4x8 slice. The times are simulated.
256 devices in a mesh: section: 8 (over z), expert: 16 (over y, x), dp: 2 (over core).
Axes of the slice: x: 4, y: 4, z: 8, core: 2. Of those that a mesh axis runs over, the one named last changes fastest.
Arguments:
- acts: bfloat16 [8, 3, 2048, 1024], P('section', None, ('expert', 'dp')), may hold values from -6 to 6
- out_grad: bfloat16 [3, 2048, 1024], P(None, ('expert', 'dp')), may hold values from -6 to 6
- ln_gain: float32 [8, 1024], P('section'), may hold values from 0.1 to 1.9
- router: bfloat16 [8, 1024, 16], P('section'), may hold values from -0.1875 to 0.1875
- w_in: bfloat16 [8, 16, 1024, 4096], P('section', 'expert', None, 'dp'), may hold values from -0.1875 to 0.1875
- w_out: bfloat16 [8, 16, 4096, 1024], P('section', 'expert', 'dp'), may hold values from -0.09375 to 0.09375
- expert_ids: int32 [8, 3, 2048, 2], P('section', None, ('expert', 'dp')), may hold values from 0 to 15, as said below
- slot_ids: int32 [8, 3, 2048, 2], P('section', None, ('expert', 'dp')), may hold values from 0 to 9, as said below
- capacity: int32 [8, 3, 16], P('section'), may hold values from 5 to 10
Outputs:
- in_grads: bfloat16 [8, 3, 2048, 1024], P('section', None, ('expert', 'dp'))
- gain_grad: float32 [8, 1024], P('section')
- router_grad: float32 [8, 1024, 16], P('section')
Inputs may be any that keep to these rules, and one draw needn't show every extreme that they name: `expert_ids`: A token's two experts differ. `slot_ids`: within one block, micro-batch and aligned block of 64 tokens (the tokens of one device), the choices that name one expert hold the slots 0, 1, 2, ... without gaps, at most 10 of them; in every block and micro-batch one expert has 10 choices from every aligned block and capacity 10.
All inputs are finite; a program needn't handle non-finite values.
Results may differ from a plain program's by a relative error of at most 0.03.
Values may be sent and summed in bfloat16 or wider, within the bound.
A program may use at most 128 MiB of HBM per device.

v0:
```python
import math
import jax
import jax.numpy as jnp
from jax import lax
from jax.sharding import PartitionSpec as P

GELU_C = math.sqrt(2.0 / math.pi)
PRECISE = lax.Precision.HIGHEST


def from_behind(shard, axis, by):
    count = lax.axis_size(axis)
    pairs = [(i, i + by) for i in range(count) if 0 <= i + by < count]
    return lax.ppermute(shard, axis, pairs)


def gelu_pair(hidden):
    inner_arg = GELU_C * (hidden + 0.044715 * hidden * hidden * hidden)
    tanh_val = jnp.tanh(inner_arg)
    active = 0.5 * hidden * (1.0 + tanh_val)
    gelu_slope = 0.5 * (1.0 + tanh_val) + 0.5 * hidden * (1.0 - tanh_val * tanh_val) * GELU_C * (
        1.0 + 3.0 * 0.044715 * hidden * hidden
    )
    return (active, gelu_slope)


def token_forward(inputs, norm_scale_weight, router_w):
    values = inputs.astype(jnp.float32)
    centred = values - jnp.mean(values, axis=-1, keepdims=True)
    inverse_deviation = lax.rsqrt(jnp.mean(centred * centred, axis=-1, keepdims=True) + 1e-06)
    expert_unit_rows = centred * inverse_deviation
    normed = (expert_unit_rows * norm_scale_weight).astype(jnp.bfloat16)
    logits = jnp.dot(normed, router_w, preferred_element_type=jnp.float32)
    return (expert_unit_rows, inverse_deviation, normed, logits)


def gate_pair(chosen):
    first_gate = 1.0 / (1.0 + jnp.exp(chosen[:, 1] - chosen[:, 0]))
    return jnp.stack([first_gate, 1.0 - first_gate], axis=1)


def token_backward(
    grad_out,
    expert_unit_rows,
    inverse_deviation,
    normed,
    norm_scale_weight,
    router_w,
    gate_vals,
    pick_table,
    gate_dots,
    expert_part,
):
    gate_diff = gate_vals[:, 0] * gate_vals[:, 1] * (gate_dots[:, 0] - gate_dots[:, 1])
    dlogits = gate_diff[:, None] * (pick_table[:, 0, :] - pick_table[:, 1, :])
    norm_gradient = expert_part + jnp.dot(
        dlogits, router_w.astype(jnp.float32).T, precision=PRECISE
    )
    router_term = jnp.dot(normed.astype(jnp.float32).T, dlogits, precision=PRECISE)
    gain_term = jnp.sum(norm_gradient * expert_unit_rows, axis=0)
    normalized_input_gradient = norm_gradient * norm_scale_weight
    input_gradient = inverse_deviation * (
        normalized_input_gradient
        - jnp.mean(normalized_input_gradient, axis=-1, keepdims=True)
        - expert_unit_rows
        * jnp.mean(normalized_input_gradient * expert_unit_rows, axis=-1, keepdims=True)
    )
    in_grad = (grad_out.astype(jnp.float32) + input_gradient).astype(jnp.bfloat16)
    return (in_grad, gain_term, router_term)


def expert_terms(rows_u, rows_grad, first_proj, second_proj):
    hidden = jnp.dot(rows_u, first_proj, preferred_element_type=jnp.float32)
    active, gelu_slope = gelu_pair(hidden)
    back_grad = lax.dot_general(
        rows_grad, second_proj, (((1,), (1,)), ((), ())), preferred_element_type=jnp.float32
    )
    gate_part = jnp.sum(active * back_grad, axis=-1)
    pre_grad = (back_grad * gelu_slope).astype(jnp.bfloat16)
    slot_part = lax.dot_general(
        pre_grad, first_proj, (((1,), (1,)), ((), ())), preferred_element_type=jnp.float32
    )
    return (slot_part, gate_part)


def per_device(acts, out_grad, ln_gain, router, w_in, w_out, expert_ids, slot_ids, capacity):
    section_count = lax.axis_size("section")
    section_index = lax.axis_index("section")
    microbatch_count = acts.shape[1]
    tok_rows = acts.shape[2]
    model_width = acts.shape[3]
    experts = router.shape[2]
    top_count = expert_ids.shape[3]
    cap_slots = 5 * tok_rows * top_count // (4 * experts)
    slot_count = experts * cap_slots
    tokens_all = tok_rows * lax.axis_size("expert") * lax.axis_size("dp")
    grad_scale = 1.0 / math.sqrt(microbatch_count * tokens_all)
    norm_scale_weight = ln_gain[0]
    router_w = router[0]
    first_proj = w_in[0, 0]
    second_proj = w_out[0, 0]
    positions = jnp.arange(slot_count, dtype=jnp.int32)
    columns = jnp.arange(experts, dtype=jnp.int32)
    section_acts = acts[0]
    section_ids = expert_ids[0]
    section_slots = slot_ids[0]
    section_caps = capacity[0]

    def run_experts(recv_u, recv_grad, is_valid):
        lead_rows = recv_u.shape[0]
        flat_u = recv_u.reshape(lead_rows * cap_slots, model_width)
        flat_grad = recv_grad.reshape(lead_rows * cap_slots, model_width)

        def expert_work(packed):
            return expert_terms(packed[0], packed[1], first_proj, second_proj)

        def skip_work(packed):
            return (
                jnp.zeros(packed[0].shape, jnp.float32),
                jnp.zeros(packed[0].shape[:1], jnp.float32),
            )

        slot_part, gate_part = lax.cond(is_valid, expert_work, skip_work, (flat_u, flat_grad))
        return (
            slot_part.reshape(lead_rows, cap_slots, model_width),
            gate_part.reshape(lead_rows, cap_slots),
        )

    def step_fn(step_index, loop_state):
        incoming, grads_acc, gain_acc, router_acc = loop_state
        micro_index = step_index - (section_count - 1 - section_index)
        is_valid = jnp.logical_and(micro_index >= 0, micro_index < microbatch_count)
        picked = jnp.clip(micro_index, 0, microbatch_count - 1)
        last_grad = lax.dynamic_index_in_dim(out_grad, picked, 0, keepdims=False)
        grad_out = jnp.where(section_index == section_count - 1, last_grad, incoming)
        inputs_now = lax.dynamic_index_in_dim(section_acts, picked, 0, keepdims=False)
        ids_now = lax.dynamic_index_in_dim(section_ids, picked, 0, keepdims=False)
        slots_now = lax.dynamic_index_in_dim(section_slots, picked, 0, keepdims=False)
        caps_now = lax.dynamic_index_in_dim(section_caps, picked, 0, keepdims=False)
        expert_unit_rows, inverse_deviation, normed, logits = token_forward(
            inputs_now, norm_scale_weight, router_w
        )
        pick_bool = ids_now[:, :, None] == columns
        pick_table = pick_bool.astype(jnp.float32)
        chosen = jnp.sum(pick_table * logits[:, None, :], axis=2)
        gate_vals = gate_pair(chosen)
        cap_sel = jnp.sum(jnp.where(pick_bool, caps_now, 0), axis=2)
        kept_mask = slots_now < cap_sel
        target = jnp.where(kept_mask, ids_now * cap_slots + slots_now, -1)
        send_map = jnp.any(positions[:, None, None] == target[None, :, :], axis=2).astype(
            jnp.bfloat16
        )
        sent_u = (
            jnp.dot(send_map, normed, preferred_element_type=jnp.float32)
            .astype(jnp.bfloat16)
            .reshape(experts, cap_slots, model_width)
        )
        sent_grad = (
            jnp.dot(send_map, grad_out, preferred_element_type=jnp.float32)
            .astype(jnp.bfloat16)
            .reshape(experts, cap_slots, model_width)
        )
        recv_u, recv_grad = (
            lax.all_to_all(sent_u, "expert", split_axis=0, concat_axis=0, tiled=True),
            lax.all_to_all(sent_grad, "expert", split_axis=0, concat_axis=0, tiled=True),
        )
        both_u, both_grad = (
            lax.all_gather(recv_u, "dp", axis=0, tiled=True),
            lax.all_gather(recv_grad, "dp", axis=0, tiled=True),
        )
        slot_part, gate_part = run_experts(both_u, both_grad, is_valid)
        summed_u, summed_g = (
            lax.psum_scatter(slot_part, "dp", scatter_dimension=0, tiled=True),
            lax.psum_scatter(gate_part, "dp", scatter_dimension=0, tiled=True),
        )
        ret_u, ret_g = (
            lax.all_to_all(
                summed_u.astype(jnp.bfloat16), "expert", split_axis=0, concat_axis=0, tiled=True
            ),
            lax.all_to_all(
                summed_g.astype(jnp.bfloat16), "expert", split_axis=0, concat_axis=0, tiled=True
            ),
        )
        flat_ret = ret_u.reshape(slot_count, model_width).astype(jnp.float32)
        flat_gate = ret_g.reshape(slot_count).astype(jnp.float32)
        hit_table = (target[:, :, None] == positions).astype(jnp.float32)
        mix_table = jnp.sum(hit_table * gate_vals[:, :, None], axis=1)
        expert_part = jnp.dot(mix_table, flat_ret, precision=PRECISE)
        gate_dots = jnp.sum(hit_table * flat_gate, axis=2)
        in_grad, gain_term, router_term = token_backward(
            grad_out,
            expert_unit_rows,
            inverse_deviation,
            normed,
            norm_scale_weight,
            router_w,
            gate_vals,
            pick_table,
            gate_dots,
            expert_part,
        )
        grads_acc = jnp.where(
            is_valid, lax.dynamic_update_index_in_dim(grads_acc, in_grad, picked, 0), grads_acc
        )
        gain_acc = gain_acc + jnp.where(is_valid, gain_term, 0.0)
        router_acc = router_acc + jnp.where(is_valid, router_term, 0.0)
        outgoing = from_behind(in_grad, "section", -1)
        return (outgoing, grads_acc, gain_acc, router_acc)

    start_state = (
        jnp.zeros((tok_rows, model_width), jnp.bfloat16),
        jnp.zeros((microbatch_count, tok_rows, model_width), jnp.bfloat16),
        jnp.zeros((model_width,), jnp.float32),
        jnp.zeros((model_width, experts), jnp.float32),
    )
    final_state = lax.fori_loop(0, microbatch_count + section_count - 1, step_fn, start_state)
    grads_acc = final_state[1]
    gain_acc, router_acc = (
        lax.psum(final_state[2].astype(jnp.bfloat16), ("expert", "dp")).astype(jnp.float32),
        lax.psum(final_state[3].astype(jnp.bfloat16), ("expert", "dp")).astype(jnp.float32),
    )
    return (grads_acc[None], (gain_acc * grad_scale)[None], (router_acc * grad_scale)[None])


def solution(mesh):
    return jax.shard_map(
        per_device,
        mesh=mesh,
        in_specs=(
            P("section", None, ("expert", "dp"), None),
            P(None, ("expert", "dp"), None),
            P("section", None),
            P("section", None, None),
            P("section", "expert", None, "dp"),
            P("section", "expert", "dp", None),
            P("section", None, ("expert", "dp"), None),
            P("section", None, ("expert", "dp"), None),
            P("section", None, None),
        ),
        out_specs=(
            P("section", None, ("expert", "dp"), None),
            P("section", None),
            P("section", None, None),
        ),
        check_vma=False,
    )
```

profile of v0, /device:TPU:96, one launch (start us, length us, event | category | flops | bytes accessed | tf_op | source)
XLA Modules:
  0.0 1215.3 jit_solution(11664580615775685706)
XLA Ops:
  7.9 1075.4 %while.23 = (s32[]{:T(128)}, bf16[64,1024]{1,0:T(8,128)(2,1)S(1)}, bf16[3,64,1024]{2,1,0:T(8,128)(2,1)S(1)}, f32[1024]{0:T(1024)S(1)}, f32[1024,16]{0,1:T(8,128)...) while((s32[]{:T(128)}, bf16[64,1024]{1,0:T(8,128)(2,1)S(1)}, ...), condition=%wide.region_16.17_spmd.clone.clone, body=%wide.region_0.16_spmd.clone.clone.sunk | while | flops 4244209152 | bytes 89025160 | solution.py:216
  22.2 10.3 all-to-all-done.1
  38.6 8.0 all-to-all-done
  52.6 21.0 %reduce-scatter.3.cloned.1.call-done = f32[16,10]{1,0:T(8,128)} async-done(((f32[32,10]{1,0:T(8,128)}), f32[16,10]{1,0:T(8,128)}) %reduce-scatter.3.cloned.1.call-update) | async-done | bytes 656 | tf_op jit(solution)/shard_map/while/body/eval_jaxpr/reduce_scatter | solution.py:174
  81.8 7.5 all-to-all-done.2
  101.9 11.4 all-to-all-done.3
  132.9 8.9 all-to-all-done.1
  147.9 7.6 all-to-all-done
  161.5 19.3 %reduce-scatter.3.cloned.1.call-done = f32[16,10]{1,0:T(8,128)} async-done(((f32[32,10]{1,0:T(8,128)}), f32[16,10]{1,0:T(8,128)}) %reduce-scatter.3.cloned.1.call-update) | async-done | bytes 656 | tf_op jit(solution)/shard_map/while/body/eval_jaxpr/reduce_scatter | solution.py:174
  188.9 7.5 all-to-all-done.2
  208.9 11.4 all-to-all-done.3
  239.9 8.9 all-to-all-done.1
  254.9 7.6 all-to-all-done
  268.5 20.0 %reduce-scatter.3.cloned.1.call-done = f32[16,10]{1,0:T(8,128)} async-done(((f32[32,10]{1,0:T(8,128)}), f32[16,10]{1,0:T(8,128)}) %reduce-scatter.3.cloned.1.call-update) | async-done | bytes 656 | tf_op jit(solution)/shard_map/while/body/eval_jaxpr/reduce_scatter | solution.py:174
  296.6 7.5 all-to-all-done.2
  316.6 11.4 all-to-all-done.3
  347.6 8.9 all-to-all-done.1
  362.6 7.6 all-to-all-done
  376.2 20.8 %reduce-scatter.3.cloned.1.call-done = f32[16,10]{1,0:T(8,128)} async-done(((f32[32,10]{1,0:T(8,128)}), f32[16,10]{1,0:T(8,128)}) %reduce-scatter.3.cloned.1.call-update) | async-done | bytes 656 | tf_op jit(solution)/shard_map/while/body/eval_jaxpr/reduce_scatter | solution.py:174
  405.2 7.5 all-to-all-done.2
  425.3 11.4 all-to-all-done.3
  456.3 8.9 all-to-all-done.1
  471.3 7.6 all-to-all-done
  481.3 14.4 %conditional.4 = (f32[320,1024]{1,0:T(8,128)S(1)}, f32[320]{0:T(512)S(1)}) conditional(s32[]{:T(128)} %convert_element_type.282, () %tuple.80, (bf16[32,10,1024]{2,0,1:T(8,128)(2,1)S(1)}, bf16[2048,1024]{1,0:T(8,128)(2,1)}, bf16[32,10,1024]{2,0,1:T(8,128)(2,1)S(1)}, bf16[1024,2048]{1,0:T(8,128)(2,1)}) %tuple.81), branch_computations={%region_7.7_spmd, %region_8.9_spmd} | conditional | flops 4045537024 | bytes 60818760 | solution.py:123
  513.9 7.5 all-to-all-done.2
  533.9 11.4 all-to-all-done.3
  564.8 8.9 all-to-all-done.1
  579.8 7.6 all-to-all-done
  589.9 14.4 %conditional.4 = (f32[320,1024]{1,0:T(8,128)S(1)}, f32[320]{0:T(512)S(1)}) conditional(s32[]{:T(128)} %convert_element_type.282, () %tuple.80, (bf16[32,10,1024]{2,0,1:T(8,128)(2,1)S(1)}, bf16[2048,1024]{1,0:T(8,128)(2,1)}, bf16[32,10,1024]{2,0,1:T(8,128)(2,1)S(1)}, bf16[1024,2048]{1,0:T(8,128)(2,1)}) %tuple.81), branch_computations={%region_7.7_spmd, %region_8.9_spmd} | conditional | flops 4045537024 | bytes 60818760 | solution.py:123
  622.4 7.5 all-to-all-done.2
  642.4 11.4 all-to-all-done.3
  673.4 8.9 all-to-all-done.1
  688.4 7.6 all-to-all-done
  698.4 14.4 %conditional.4 = (f32[320,1024]{1,0:T(8,128)S(1)}, f32[320]{0:T(512)S(1)}) conditional(s32[]{:T(128)} %convert_element_type.282, () %tuple.80, (bf16[32,10,1024]{2,0,1:T(8,128)(2,1)S(1)}, bf16[2048,1024]{1,0:T(8,128)(2,1)}, bf16[32,10,1024]{2,0,1:T(8,128)(2,1)S(1)}, bf16[1024,2048]{1,0:T(8,128)(2,1)}) %tuple.81), branch_computations={%region_7.7_spmd, %region_8.9_spmd} | conditional | flops 4045537024 | bytes 60818760 | solution.py:123
  750.0 11.4 all-to-all-done.3
  781.0 8.9 all-to-all-done.1
  796.0 7.6 all-to-all-done
  809.6 17.6 %reduce-scatter.3.cloned.1.call-done = f32[16,10]{1,0:T(8,128)} async-done(((f32[32,10]{1,0:T(8,128)}), f32[16,10]{1,0:T(8,128)}) %reduce-scatter.3.cloned.1.call-update) | async-done | bytes 656 | tf_op jit(solution)/shard_map/while/body/eval_jaxpr/reduce_scatter | solution.py:174
  855.3 11.4 all-to-all-done.3
  886.3 8.9 all-to-all-done.1
  901.3 7.6 all-to-all-done
  914.9 16.6 %reduce-scatter.3.cloned.1.call-done = f32[16,10]{1,0:T(8,128)} async-done(((f32[32,10]{1,0:T(8,128)}), f32[16,10]{1,0:T(8,128)}) %reduce-scatter.3.cloned.1.call-update) | async-done | bytes 656 | tf_op jit(solution)/shard_map/while/body/eval_jaxpr/reduce_scatter | solution.py:174
  959.7 11.4 all-to-all-done.3
  990.7 8.9 all-to-all-done.1
  1005.7 7.6 all-to-all-done
  1019.3 15.7 %reduce-scatter.3.cloned.1.call-done = f32[16,10]{1,0:T(8,128)} async-done(((f32[32,10]{1,0:T(8,128)}), f32[16,10]{1,0:T(8,128)}) %reduce-scatter.3.cloned.1.call-update) | async-done | bytes 656 | tf_op jit(solution)/shard_map/while/body/eval_jaxpr/reduce_scatter | solution.py:174
  1063.1 11.4 all-to-all-done.3
  1083.3 123.8 %all-reduce = (bf16[1024]{0:T(1024)(128)(2,1)S(1)}, bf16[1024,16]{0,1:T(8,128)(2,1)S(1)}) all-reduce(bf16[1024]{0:T(1024)(128)(2,1)S(1)} %convert_element_type.153, bf16[1024,16]{0,1:T(8,128)(2,1)S(1)} %convert_element_type.155), channel_id=1, replica_groups=mesh['section'=8,'expert'=16,'dp'=2] {'expert','dp'}, use_global_device_ids=true, to_apply=%region_17.18 | all-reduce | flops 17408 | bytes 69632 | tf_op jit(solution)/shard_map/psum | solution.py:219
  (652 shorter events, 618.9 us)
Async XLA Ops:
  13.9 18.6 %all-to-all-start.1 = ((bf16[16,10,1024]{2,1,0:T(8,128)(2,1)}), bf16[16,10,1024]{2,1,0:T(8,128)(2,1)S(1)}, u32[]{:S(2)}, u32[]{:S(2)}) async-start(bf16[16,10,1024]{2,1,0:T(8,128)(2,1)} %reshape.239), calls=%async_computation.1 | async-start | bytes 1048576 | tf_op jit(solution)/shard_map/while/body/eval_jaxpr/all_to_all | solution.py:164
  32.5 14.1 %all-to-all-start = ((bf16[16,10,1024]{2,1,0:T(8,128)(2,1)}), bf16[16,10,1024]{2,1,0:T(8,128)(2,1)S(1)}, u32[]{:S(2)}, u32[]{:S(2)}) async-start(bf16[16,10,1024]{2,1,0:T(8,128)(2,1)} %reshape.238), calls=%async_computation | async-start | bytes 1048576 | tf_op jit(solution)/shard_map/while/body/eval_jaxpr/all_to_all | solution.py:165
  36.1 37.6 %reduce-scatter.3.cloned.1.call-start = ((), (), s32[]{:S(2)}) async-start(), calls=%async_computation.6 | async-start | bytes 24576 | tf_op jit(solution)/shard_map/while/body/eval_jaxpr/reduce_scatter | solution.py:174
  50.0 42.5 %reduce-scatter.5.cloned.1.call-start = ((), (), s32[]{:S(2)}) async-start(), calls=%async_computation.7 | async-start | bytes 3145728 | tf_op jit(solution)/shard_map/while/body/eval_jaxpr/reduce_scatter | solution.py:173
  75.0 14.3 %all-to-all-start.2 = ((bf16[16,1,10]{2,1,0:T(2,128)(2,1)}), bf16[16,1,10]{2,1,0:T(2,128)(2,1)S(1)}, u32[]{:S(2)}, u32[]{:S(2)}) async-start(bf16[16,1,10]{2,1,0:T(2,128)(2,1)} %copy.45), calls=%async_computation.3 | async-start | bytes 16384 | tf_op jit(solution)/shard_map/while/body/eval_jaxpr/all_to_all | solution.py:180
  94.5 18.8 %all-to-all-start.3 = ((bf16[16,10,1024]{2,1,0:T(8,128)(2,1)}), bf16[16,10,1024]{2,1,0:T(8,128)(2,1)S(1)}, u32[]{:S(2)}, u32[]{:S(2)}) async-start(bf16[16,10,1024]{2,1,0:T(8,128)(2,1)} %convert_element_type.283), calls=%async_computation.5 | async-start | bytes 1048576 | tf_op jit(solution)/shard_map/while/body/eval_jaxpr/all_to_all | solution.py:177
  141.8 13.7 %all-to-all-start = ((bf16[16,10,1024]{2,1,0:T(8,128)(2,1)}), bf16[16,10,1024]{2,1,0:T(8,128)(2,1)S(1)}, u32[]{:S(2)}, u32[]{:S(2)}) async-start(bf16[16,10,1024]{2,1,0:T(8,128)(2,1)} %reshape.238), calls=%async_computation | async-start | bytes 1048576 | tf_op jit(solution)/shard_map/while/body/eval_jaxpr/all_to_all | solution.py:165
  145.4 35.4 %reduce-scatter.3.cloned.1.call-start = ((), (), s32[]{:S(2)}) async-start(), calls=%async_computation.6 | async-start | bytes 24576 | tf_op jit(solution)/shard_map/while/body/eval_jaxpr/reduce_scatter | solution.py:174
  158.8 40.5 %reduce-scatter.5.cloned.1.call-start = ((), (), s32[]{:S(2)}) async-start(), calls=%async_computation.7 | async-start | bytes 3145728 | tf_op jit(solution)/shard_map/while/body/eval_jaxpr/reduce_scatter | solution.py:173
  182.1 14.3 %all-to-all-start.2 = ((bf16[16,1,10]{2,1,0:T(2,128)(2,1)}), bf16[16,1,10]{2,1,0:T(2,128)(2,1)S(1)}, u32[]{:S(2)}, u32[]{:S(2)}) async-start(bf16[16,1,10]{2,1,0:T(2,128)(2,1)} %copy.45), calls=%async_computation.3 | async-start | bytes 16384 | tf_op jit(solution)/shard_map/while/body/eval_jaxpr/all_to_all | solution.py:180
  201.5 18.8 %all-to-all-start.3 = ((bf16[16,10,1024]{2,1,0:T(8,128)(2,1)}), bf16[16,10,1024]{2,1,0:T(8,128)(2,1)S(1)}, u32[]{:S(2)}, u32[]{:S(2)}) async-start(bf16[16,10,1024]{2,1,0:T(8,128)(2,1)} %convert_element_type.283), calls=%async_computation.5 | async-start | bytes 1048576 | tf_op jit(solution)/shard_map/while/body/eval_jaxpr/all_to_all | solution.py:177
  248.8 13.7 %all-to-all-start = ((bf16[16,10,1024]{2,1,0:T(8,128)(2,1)}), bf16[16,10,1024]{2,1,0:T(8,128)(2,1)S(1)}, u32[]{:S(2)}, u32[]{:S(2)}) async-start(bf16[16,10,1024]{2,1,0:T(8,128)(2,1)} %reshape.238), calls=%async_computation | async-start | bytes 1048576 | tf_op jit(solution)/shard_map/while/body/eval_jaxpr/all_to_all | solution.py:165
  252.3 36.1 %reduce-scatter.3.cloned.1.call-start = ((), (), s32[]{:S(2)}) async-start(), calls=%async_computation.6 | async-start | bytes 24576 | tf_op jit(solution)/shard_map/while/body/eval_jaxpr/reduce_scatter | solution.py:174
  265.8 41.3 %reduce-scatter.5.cloned.1.call-start = ((), (), s32[]{:S(2)}) async-start(), calls=%async_computation.7 | async-start | bytes 3145728 | tf_op jit(solution)/shard_map/while/body/eval_jaxpr/reduce_scatter | solution.py:173
  289.8 14.3 %all-to-all-start.2 = ((bf16[16,1,10]{2,1,0:T(2,128)(2,1)}), bf16[16,1,10]{2,1,0:T(2,128)(2,1)S(1)}, u32[]{:S(2)}, u32[]{:S(2)}) async-start(bf16[16,1,10]{2,1,0:T(2,128)(2,1)} %copy.45), calls=%async_computation.3 | async-start | bytes 16384 | tf_op jit(solution)/shard_map/while/body/eval_jaxpr/all_to_all | solution.py:180
  309.2 18.8 %all-to-all-start.3 = ((bf16[16,10,1024]{2,1,0:T(8,128)(2,1)}), bf16[16,10,1024]{2,1,0:T(8,128)(2,1)S(1)}, u32[]{:S(2)}, u32[]{:S(2)}) async-start(bf16[16,10,1024]{2,1,0:T(8,128)(2,1)} %convert_element_type.283), calls=%async_computation.5 | async-start | bytes 1048576 | tf_op jit(solution)/shard_map/while/body/eval_jaxpr/all_to_all | solution.py:177
  356.5 13.7 %all-to-all-start = ((bf16[16,10,1024]{2,1,0:T(8,128)(2,1)}), bf16[16,10,1024]{2,1,0:T(8,128)(2,1)S(1)}, u32[]{:S(2)}, u32[]{:S(2)}) async-start(bf16[16,10,1024]{2,1,0:T(8,128)(2,1)} %reshape.238), calls=%async_computation | async-start | bytes 1048576 | tf_op jit(solution)/shard_map/while/body/eval_jaxpr/all_to_all | solution.py:165
  360.1 37.0 %reduce-scatter.3.cloned.1.call-start = ((), (), s32[]{:S(2)}) async-start(), calls=%async_computation.6 | async-start | bytes 24576 | tf_op jit(solution)/shard_map/while/body/eval_jaxpr/reduce_scatter | solution.py:174
  373.5 42.3 %reduce-scatter.5.cloned.1.call-start = ((), (), s32[]{:S(2)}) async-start(), calls=%async_computation.7 | async-start | bytes 3145728 | tf_op jit(solution)/shard_map/while/body/eval_jaxpr/reduce_scatter | solution.py:173
  398.3 14.3 %all-to-all-start.2 = ((bf16[16,1,10]{2,1,0:T(2,128)(2,1)}), bf16[16,1,10]{2,1,0:T(2,128)(2,1)S(1)}, u32[]{:S(2)}, u32[]{:S(2)}) async-start(bf16[16,1,10]{2,1,0:T(2,128)(2,1)} %copy.45), calls=%async_computation.3 | async-start | bytes 16384 | tf_op jit(solution)/shard_map/while/body/eval_jaxpr/all_to_all | solution.py:180
  417.9 18.8 %all-to-all-start.3 = ((bf16[16,10,1024]{2,1,0:T(8,128)(2,1)}), bf16[16,10,1024]{2,1,0:T(8,128)(2,1)S(1)}, u32[]{:S(2)}, u32[]{:S(2)}) async-start(bf16[16,10,1024]{2,1,0:T(8,128)(2,1)} %convert_element_type.283), calls=%async_computation.5 | async-start | bytes 1048576 | tf_op jit(solution)/shard_map/while/body/eval_jaxpr/all_to_all | solution.py:177
  465.2 13.7 %all-to-all-start = ((bf16[16,10,1024]{2,1,0:T(8,128)(2,1)}), bf16[16,10,1024]{2,1,0:T(8,128)(2,1)S(1)}, u32[]{:S(2)}, u32[]{:S(2)}) async-start(bf16[16,10,1024]{2,1,0:T(8,128)(2,1)} %reshape.238), calls=%async_computation | async-start | bytes 1048576 | tf_op jit(solution)/shard_map/while/body/eval_jaxpr/all_to_all | solution.py:165
  468.8 37.0 %reduce-scatter.3.cloned.1.call-start = ((), (), s32[]{:S(2)}) async-start(), calls=%async_computation.6 | async-start | bytes 24576 | tf_op jit(solution)/shard_map/while/body/eval_jaxpr/reduce_scatter | solution.py:174
  496.4 27.9 %reduce-scatter.5.cloned.1.call-start = ((), (), s32[]{:S(2)}) async-start(), calls=%async_computation.7 | async-start | bytes 3145728 | tf_op jit(solution)/shard_map/while/body/eval_jaxpr/reduce_scatter | solution.py:173
  507.0 14.3 %all-to-all-start.2 = ((bf16[16,1,10]{2,1,0:T(2,128)(2,1)}), bf16[16,1,10]{2,1,0:T(2,128)(2,1)S(1)}, u32[]{:S(2)}, u32[]{:S(2)}) async-start(bf16[16,1,10]{2,1,0:T(2,128)(2,1)} %copy.45), calls=%async_computation.3 | async-start | bytes 16384 | tf_op jit(solution)/shard_map/while/body/eval_jaxpr/all_to_all | solution.py:180
  526.4 18.8 %all-to-all-start.3 = ((bf16[16,10,1024]{2,1,0:T(8,128)(2,1)}), bf16[16,10,1024]{2,1,0:T(8,128)(2,1)S(1)}, u32[]{:S(2)}, u32[]{:S(2)}) async-start(bf16[16,10,1024]{2,1,0:T(8,128)(2,1)} %convert_element_type.283), calls=%async_computation.5 | async-start | bytes 1048576 | tf_op jit(solution)/shard_map/while/body/eval_jaxpr/all_to_all | solution.py:177
  577.3 37.0 %reduce-scatter.3.cloned.1.call-start = ((), (), s32[]{:S(2)}) async-start(), calls=%async_computation.6 | async-start | bytes 24576 | tf_op jit(solution)/shard_map/while/body/eval_jaxpr/reduce_scatter | solution.py:174
  605.0 27.9 %reduce-scatter.5.cloned.1.call-start = ((), (), s32[]{:S(2)}) async-start(), calls=%async_computation.7 | async-start | bytes 3145728 | tf_op jit(solution)/shard_map/while/body/eval_jaxpr/reduce_scatter | solution.py:173
  615.6 14.3 %all-to-all-start.2 = ((bf16[16,1,10]{2,1,0:T(2,128)(2,1)}), bf16[16,1,10]{2,1,0:T(2,128)(2,1)S(1)}, u32[]{:S(2)}, u32[]{:S(2)}) async-start(bf16[16,1,10]{2,1,0:T(2,128)(2,1)} %copy.45), calls=%async_computation.3 | async-start | bytes 16384 | tf_op jit(solution)/shard_map/while/body/eval_jaxpr/all_to_all | solution.py:180
  635.0 18.8 %all-to-all-start.3 = ((bf16[16,10,1024]{2,1,0:T(8,128)(2,1)}), bf16[16,10,1024]{2,1,0:T(8,128)(2,1)S(1)}, u32[]{:S(2)}, u32[]{:S(2)}) async-start(bf16[16,10,1024]{2,1,0:T(8,128)(2,1)} %convert_element_type.283), calls=%async_computation.5 | async-start | bytes 1048576 | tf_op jit(solution)/shard_map/while/body/eval_jaxpr/all_to_all | solution.py:177
  682.3 13.7 %all-to-all-start = ((bf16[16,10,1024]{2,1,0:T(8,128)(2,1)}), bf16[16,10,1024]{2,1,0:T(8,128)(2,1)S(1)}, u32[]{:S(2)}, u32[]{:S(2)}) async-start(bf16[16,10,1024]{2,1,0:T(8,128)(2,1)} %reshape.238), calls=%async_computation | async-start | bytes 1048576 | tf_op jit(solution)/shard_map/while/body/eval_jaxpr/all_to_all | solution.py:165
  685.9 36.0 %reduce-scatter.3.cloned.1.call-start = ((), (), s32[]{:S(2)}) async-start(), calls=%async_computation.6 | async-start | bytes 24576 | tf_op jit(solution)/shard_map/while/body/eval_jaxpr/reduce_scatter | solution.py:174
  713.6 26.9 %reduce-scatter.5.cloned.1.call-start = ((), (), s32[]{:S(2)}) async-start(), calls=%async_computation.7 | async-start | bytes 3145728 | tf_op jit(solution)/shard_map/while/body/eval_jaxpr/reduce_scatter | solution.py:173
  723.1 14.3 %all-to-all-start.2 = ((bf16[16,1,10]{2,1,0:T(2,128)(2,1)}), bf16[16,1,10]{2,1,0:T(2,128)(2,1)S(1)}, u32[]{:S(2)}, u32[]{:S(2)}) async-start(bf16[16,1,10]{2,1,0:T(2,128)(2,1)} %copy.45), calls=%async_computation.3 | async-start | bytes 16384 | tf_op jit(solution)/shard_map/while/body/eval_jaxpr/all_to_all | solution.py:180
  742.6 18.8 %all-to-all-start.3 = ((bf16[16,10,1024]{2,1,0:T(8,128)(2,1)}), bf16[16,10,1024]{2,1,0:T(8,128)(2,1)S(1)}, u32[]{:S(2)}, u32[]{:S(2)}) async-start(bf16[16,10,1024]{2,1,0:T(8,128)(2,1)} %convert_element_type.283), calls=%async_computation.5 | async-start | bytes 1048576 | tf_op jit(solution)/shard_map/while/body/eval_jaxpr/all_to_all | solution.py:177
  793.4 33.8 %reduce-scatter.3.cloned.1.call-start = ((), (), s32[]{:S(2)}) async-start(), calls=%async_computation.6 | async-start | bytes 24576 | tf_op jit(solution)/shard_map/while/body/eval_jaxpr/reduce_scatter | solution.py:174
  806.9 38.9 %reduce-scatter.5.cloned.1.call-start = ((), (), s32[]{:S(2)}) async-start(), calls=%async_computation.7 | async-start | bytes 3145728 | tf_op jit(solution)/shard_map/while/body/eval_jaxpr/reduce_scatter | solution.py:173
  828.5 14.3 %all-to-all-start.2 = ((bf16[16,1,10]{2,1,0:T(2,128)(2,1)}), bf16[16,1,10]{2,1,0:T(2,128)(2,1)S(1)}, u32[]{:S(2)}, u32[]{:S(2)}) async-start(bf16[16,1,10]{2,1,0:T(2,128)(2,1)} %copy.45), calls=%async_computation.3 | async-start | bytes 16384 | tf_op jit(solution)/shard_map/while/body/eval_jaxpr/all_to_all | solution.py:180
  847.9 18.8 %all-to-all-start.3 = ((bf16[16,10,1024]{2,1,0:T(8,128)(2,1)}), bf16[16,10,1024]{2,1,0:T(8,128)(2,1)S(1)}, u32[]{:S(2)}, u32[]{:S(2)}) async-start(bf16[16,10,1024]{2,1,0:T(8,128)(2,1)} %convert_element_type.283), calls=%async_computation.5 | async-start | bytes 1048576 | tf_op jit(solution)/shard_map/while/body/eval_jaxpr/all_to_all | solution.py:177
  898.8 32.8 %reduce-scatter.3.cloned.1.call-start = ((), (), s32[]{:S(2)}) async-start(), calls=%async_computation.6 | async-start | bytes 24576 | tf_op jit(solution)/shard_map/while/body/eval_jaxpr/reduce_scatter | solution.py:174
  912.3 37.9 %reduce-scatter.5.cloned.1.call-start = ((), (), s32[]{:S(2)}) async-start(), calls=%async_computation.7 | async-start | bytes 3145728 | tf_op jit(solution)/shard_map/while/body/eval_jaxpr/reduce_scatter | solution.py:173
  932.9 14.3 %all-to-all-start.2 = ((bf16[16,1,10]{2,1,0:T(2,128)(2,1)}), bf16[16,1,10]{2,1,0:T(2,128)(2,1)S(1)}, u32[]{:S(2)}, u32[]{:S(2)}) async-start(bf16[16,1,10]{2,1,0:T(2,128)(2,1)} %copy.45), calls=%async_computation.3 | async-start | bytes 16384 | tf_op jit(solution)/shard_map/while/body/eval_jaxpr/all_to_all | solution.py:180
  952.3 18.8 %all-to-all-start.3 = ((bf16[16,10,1024]{2,1,0:T(8,128)(2,1)}), bf16[16,10,1024]{2,1,0:T(8,128)(2,1)S(1)}, u32[]{:S(2)}, u32[]{:S(2)}) async-start(bf16[16,10,1024]{2,1,0:T(8,128)(2,1)} %convert_element_type.283), calls=%async_computation.5 | async-start | bytes 1048576 | tf_op jit(solution)/shard_map/while/body/eval_jaxpr/all_to_all | solution.py:177
  999.6 13.7 %all-to-all-start = ((bf16[16,10,1024]{2,1,0:T(8,128)(2,1)}), bf16[16,10,1024]{2,1,0:T(8,128)(2,1)S(1)}, u32[]{:S(2)}, u32[]{:S(2)}) async-start(bf16[16,10,1024]{2,1,0:T(8,128)(2,1)} %reshape.238), calls=%async_computation | async-start | bytes 1048576 | tf_op jit(solution)/shard_map/while/body/eval_jaxpr/all_to_all | solution.py:165
  1003.1 31.8 %reduce-scatter.3.cloned.1.call-start = ((), (), s32[]{:S(2)}) async-start(), calls=%async_computation.6 | async-start | bytes 24576 | tf_op jit(solution)/shard_map/while/body/eval_jaxpr/reduce_scatter | solution.py:174
  1016.6 37.0 %reduce-scatter.5.cloned.1.call-start = ((), (), s32[]{:S(2)}) async-start(), calls=%async_computation.7 | async-start | bytes 3145728 | tf_op jit(solution)/shard_map/while/body/eval_jaxpr/reduce_scatter | solution.py:173
  1036.3 14.3 %all-to-all-start.2 = ((bf16[16,1,10]{2,1,0:T(2,128)(2,1)}), bf16[16,1,10]{2,1,0:T(2,128)(2,1)S(1)}, u32[]{:S(2)}, u32[]{:S(2)}) async-start(bf16[16,1,10]{2,1,0:T(2,128)(2,1)} %copy.45), calls=%async_computation.3 | async-start | bytes 16384 | tf_op jit(solution)/shard_map/while/body/eval_jaxpr/all_to_all | solution.py:180
  1055.7 18.8 %all-to-all-start.3 = ((bf16[16,10,1024]{2,1,0:T(8,128)(2,1)}), bf16[16,10,1024]{2,1,0:T(8,128)(2,1)S(1)}, u32[]{:S(2)}, u32[]{:S(2)}) async-start(bf16[16,10,1024]{2,1,0:T(8,128)(2,1)} %convert_element_type.283), calls=%async_computation.5 | async-start | bytes 1048576 | tf_op jit(solution)/shard_map/while/body/eval_jaxpr/all_to_all | solution.py:177
  (69 other events, 548.4 us)
Sparse Core Ops, SparseCore 0:
  50.1 23.5 reduce-scatter.2
  76.1 16.2 reduce-scatter.4
  159.0 21.7 reduce-scatter.2
  183.1 16.2 reduce-scatter.4
  265.9 22.5 reduce-scatter.2
  290.8 16.2 reduce-scatter.4
  373.6 23.3 reduce-scatter.2
  399.5 16.2 reduce-scatter.4
  496.6 9.1 reduce-scatter.2
  508.1 16.2 reduce-scatter.4
  605.1 9.1 reduce-scatter.2
  616.6 16.2 reduce-scatter.4
  713.7 8.1 reduce-scatter.2
  724.2 16.2 reduce-scatter.4
  807.0 20.1 reduce-scatter.2
  829.6 16.2 reduce-scatter.4
  912.4 19.1 reduce-scatter.2
  933.9 16.2 reduce-scatter.4
  1016.7 18.1 reduce-scatter.2
  1037.3 16.2 reduce-scatter.4
where the time goes:
time: 1220 us
  waiting for transfers between devices  590 us (48%)
  starting transfers between devices  236 us (19%)
  blocking collectives  169 us (14%)
  other arithmetic  71 us (6%)
  matrix products  66.8 us (5%)
  local copies, waits for them, and re-layouts  65.6 us (5%)
  between operations  14.1 us (1%)
    reduce_scatter x10, waiting for transfers between devices, step_fn(): lax.psum_scatter(gate_part, 'dp', scatter_dimension=0, tiled=True)  150 us
    psum x1, blocking collectives, per_device(): lax.psum(final_state[2].astype(jnp.bfloat16), ('expert', 'dp'))  124 us
    all_to_all x10, waiting for transfers between devices, step_fn(): lax.all_to_all(summed_u.astype(jnp.bfloat16), 'expert', split_axis=0, con...  114 us
    all_to_all x10, waiting for transfers between devices, step_fn(): lax.all_to_all(sent_u, 'expert', split_axis=0, concat_axis=0, tiled=True)  90.5 us
    all_to_all x10, waiting for transfers between devices, step_fn(): lax.all_to_all(sent_grad, 'expert', split_axis=0, concat_axis=0, tiled=True)  76.2 us
    all_to_all x10, waiting for transfers between devices, step_fn(): lax.all_to_all(summed_g.astype(jnp.bfloat16), 'expert', split_axis=0, con...  74.6 us
    all_to_all x10, starting transfers between devices, step_fn(): lax.all_to_all(summed_u.astype(jnp.bfloat16), 'expert', split_axis=0, con...  68.1 us
    all_to_all x10, starting transfers between devices, step_fn(): lax.all_to_all(summed_g.astype(jnp.bfloat16), 'expert', split_axis=0, con...  68.1 us
  transfers between devices with their start and end apart: 70, of which 70 were waited for; matrix products, arithmetic and copies ran while one was open for 5% of the time, Pallas kernels for 0%

commit v1 on v0

--- a/solution.py
+++ b/solution.py
@@ -216,7 +216,7 @@
     final_state = lax.fori_loop(0, microbatch_count + section_count - 1, step_fn, start_state)
     grads_acc = final_state[1]
     gain_acc, router_acc = (
-        lax.psum(final_state[2].astype(jnp.bfloat16), ("expert", "dp")).astype(jnp.float32),
+        lax.psum(lax.psum(final_state[2].astype(jnp.bfloat16), "expert"), "dp").astype(jnp.float32),
         lax.psum(final_state[3].astype(jnp.bfloat16), ("expert", "dp")).astype(jnp.float32),
     )
     return (grads_acc[None], (gain_acc * grad_scale)[None], (router_acc * grad_scale)[None])

time: 1220 us -> 1260 us (1.033)
  blocking collectives: 169 us -> 207 us
    psum x1 -> x3, blocking collectives: 124 us -> 162 us  [the longest x1 124 us: per_device(): lax.psum(final_state[3].astype(jnp.bfloat16), ('expert', 'dp'))]
where the time goes in v1:
time: 1260 us; the launch traced here: 1250 us
  waiting for transfers between devices  590 us (47%)
  starting transfers between devices  236 us (19%)
  blocking collectives  207 us (16%)
  other arithmetic  71 us (6%)
  matrix products  66.8 us (5%)
  local copies, waits for them, and re-layouts  65.6 us (5%)
  between operations  14 us (1%)
    reduce_scatter x10, waiting for transfers between devices, step_fn(): lax.psum_scatter(gate_part, 'dp', scatter_dimension=0, tiled=True)  150 us
    psum x1, blocking collectives, per_device(): lax.psum(final_state[3].astype(jnp.bfloat16), ('expert', 'dp'))  124 us
    all_to_all x10, waiting for transfers between devices, step_fn(): lax.all_to_all(summed_u.astype(jnp.bfloat16), 'expert', split_axis=0, con...  114 us
    all_to_all x10, waiting for transfers between devices, step_fn(): lax.all_to_all(sent_u, 'expert', split_axis=0, concat_axis=0, tiled=True)  90.5 us
    all_to_all x10, waiting for transfers between devices, step_fn(): lax.all_to_all(sent_grad, 'expert', split_axis=0, concat_axis=0, tiled=True)  76.2 us
    all_to_all x10, waiting for transfers between devices, step_fn(): lax.all_to_all(summed_g.astype(jnp.bfloat16), 'expert', split_axis=0, con...  74.6 us
    all_to_all x10, starting transfers between devices, step_fn(): lax.all_to_all(summed_u.astype(jnp.bfloat16), 'expert', split_axis=0, con...  68.1 us
    all_to_all x10, starting transfers between devices, step_fn(): lax.all_to_all(summed_g.astype(jnp.bfloat16), 'expert', split_axis=0, con...  68.1 us
  transfers between devices with their start and end apart: 70, of which 70 were waited for; matrix products, arithmetic and copies ran while one was open for 5% of the time, Pallas kernels for 0%

profile of v1, /device:TPU:96, one launch (start us, length us, event | category | flops | bytes accessed | tf_op | source)
XLA Modules:
  0.0 1253.2 jit_solution(2888642034845253042)
XLA Ops:
  7.9 1075.4 %while.23 = (s32[]{:T(128)}, bf16[64,1024]{1,0:T(8,128)(2,1)S(1)}, bf16[3,64,1024]{2,1,0:T(8,128)(2,1)S(1)}, f32[1024]{0:T(1024)S(1)}, f32[1024,16]{0,1:T(8,128)...) while((s32[]{:T(128)}, bf16[64,1024]{1,0:T(8,128)(2,1)S(1)}, ...), condition=%wide.region_16.17_spmd.clone.clone, body=%wide.region_0.16_spmd.clone.clone.sunk | while | flops 4244209152 | bytes 89025160 | solution.py:216
  22.2 10.3 all-to-all-done.1
  38.6 8.0 all-to-all-done
  52.6 21.0 %reduce-scatter.3.cloned.1.call-done = f32[16,10]{1,0:T(8,128)} async-done(((f32[32,10]{1,0:T(8,128)}), f32[16,10]{1,0:T(8,128)}) %reduce-scatter.3.cloned.1.call-update) | async-done | bytes 656 | tf_op jit(solution)/shard_map/while/body/eval_jaxpr/reduce_scatter | solution.py:174
  81.8 7.5 all-to-all-done.2
  101.9 11.4 all-to-all-done.3
  132.9 8.9 all-to-all-done.1
  147.9 7.6 all-to-all-done
  161.5 19.3 %reduce-scatter.3.cloned.1.call-done = f32[16,10]{1,0:T(8,128)} async-done(((f32[32,10]{1,0:T(8,128)}), f32[16,10]{1,0:T(8,128)}) %reduce-scatter.3.cloned.1.call-update) | async-done | bytes 656 | tf_op jit(solution)/shard_map/while/body/eval_jaxpr/reduce_scatter | solution.py:174
  188.9 7.5 all-to-all-done.2
  208.9 11.4 all-to-all-done.3
  239.9 8.9 all-to-all-done.1
  254.9 7.6 all-to-all-done
  268.5 20.0 %reduce-scatter.3.cloned.1.call-done = f32[16,10]{1,0:T(8,128)} async-done(((f32[32,10]{1,0:T(8,128)}), f32[16,10]{1,0:T(8,128)}) %reduce-scatter.3.cloned.1.call-update) | async-done | bytes 656 | tf_op jit(solution)/shard_map/while/body/eval_jaxpr/reduce_scatter | solution.py:174
  296.6 7.5 all-to-all-done.2
  316.6 11.4 all-to-all-done.3
  347.6 8.9 all-to-all-done.1
  362.6 7.6 all-to-all-done
  376.2 20.8 %reduce-scatter.3.cloned.1.call-done = f32[16,10]{1,0:T(8,128)} async-done(((f32[32,10]{1,0:T(8,128)}), f32[16,10]{1,0:T(8,128)}) %reduce-scatter.3.cloned.1.call-update) | async-done | bytes 656 | tf_op jit(solution)/shard_map/while/body/eval_jaxpr/reduce_scatter | solution.py:174
  405.2 7.5 all-to-all-done.2
  425.3 11.4 all-to-all-done.3
  456.3 8.9 all-to-all-done.1
  471.3 7.6 all-to-all-done
  481.3 14.4 %conditional.4 = (f32[320,1024]{1,0:T(8,128)S(1)}, f32[320]{0:T(512)S(1)}) conditional(s32[]{:T(128)} %convert_element_type.282, () %tuple.80, (bf16[32,10,1024]{2,0,1:T(8,128)(2,1)S(1)}, bf16[2048,1024]{1,0:T(8,128)(2,1)}, bf16[32,10,1024]{2,0,1:T(8,128)(2,1)S(1)}, bf16[1024,2048]{1,0:T(8,128)(2,1)}) %tuple.81), branch_computations={%region_7.7_spmd, %region_8.9_spmd} | conditional | flops 4045537024 | bytes 60818760 | solution.py:123
  513.9 7.5 all-to-all-done.2
  533.9 11.4 all-to-all-done.3
  564.8 8.9 all-to-all-done.1
  579.8 7.6 all-to-all-done
  589.9 14.4 %conditional.4 = (f32[320,1024]{1,0:T(8,128)S(1)}, f32[320]{0:T(512)S(1)}) conditional(s32[]{:T(128)} %convert_element_type.282, () %tuple.80, (bf16[32,10,1024]{2,0,1:T(8,128)(2,1)S(1)}, bf16[2048,1024]{1,0:T(8,128)(2,1)}, bf16[32,10,1024]{2,0,1:T(8,128)(2,1)S(1)}, bf16[1024,2048]{1,0:T(8,128)(2,1)}) %tuple.81), branch_computations={%region_7.7_spmd, %region_8.9_spmd} | conditional | flops 4045537024 | bytes 60818760 | solution.py:123
  642.4 11.4 all-to-all-done.3
  673.4 8.9 all-to-all-done.1
  688.4 7.6 all-to-all-done
  698.4 14.4 %conditional.4 = (f32[320,1024]{1,0:T(8,128)S(1)}, f32[320]{0:T(512)S(1)}) conditional(s32[]{:T(128)} %convert_element_type.282, () %tuple.80, (bf16[32,10,1024]{2,0,1:T(8,128)(2,1)S(1)}, bf16[2048,1024]{1,0:T(8,128)(2,1)}, bf16[32,10,1024]{2,0,1:T(8,128)(2,1)S(1)}, bf16[1024,2048]{1,0:T(8,128)(2,1)}) %tuple.81), branch_computations={%region_7.7_spmd, %region_8.9_spmd} | conditional | flops 4045537024 | bytes 60818760 | solution.py:123
  750.0 11.4 all-to-all-done.3
  781.0 8.9 all-to-all-done.1
  796.0 7.6 all-to-all-done
  809.6 17.6 %reduce-scatter.3.cloned.1.call-done = f32[16,10]{1,0:T(8,128)} async-done(((f32[32,10]{1,0:T(8,128)}), f32[16,10]{1,0:T(8,128)}) %reduce-scatter.3.cloned.1.call-update) | async-done | bytes 656 | tf_op jit(solution)/shard_map/while/body/eval_jaxpr/reduce_scatter | solution.py:174
  855.3 11.4 all-to-all-done.3
  886.3 8.9 all-to-all-done.1
  901.3 7.6 all-to-all-done
  914.9 16.6 %reduce-scatter.3.cloned.1.call-done = f32[16,10]{1,0:T(8,128)} async-done(((f32[32,10]{1,0:T(8,128)}), f32[16,10]{1,0:T(8,128)}) %reduce-scatter.3.cloned.1.call-update) | async-done | bytes 656 | tf_op jit(solution)/shard_map/while/body/eval_jaxpr/reduce_scatter | solution.py:174
  959.7 11.4 all-to-all-done.3
  990.7 8.9 all-to-all-done.1
  1005.7 7.6 all-to-all-done
  1019.3 15.7 %reduce-scatter.3.cloned.1.call-done = f32[16,10]{1,0:T(8,128)} async-done(((f32[32,10]{1,0:T(8,128)}), f32[16,10]{1,0:T(8,128)}) %reduce-scatter.3.cloned.1.call-update) | async-done | bytes 656 | tf_op jit(solution)/shard_map/while/body/eval_jaxpr/reduce_scatter | solution.py:174
  1063.1 11.4 all-to-all-done.3
  1083.3 123.8 %psum.23 = bf16[1024,16]{0,1:T(8,128)(2,1)S(1)} all-reduce(bf16[1024,16]{0,1:T(8,128)(2,1)S(1)} %convert_element_type.155), channel_id=1, replica_groups=mesh['section'=8,'expert'=16,'dp'=2] {'expert','dp'}, use_global_device_ids=true, to_apply=%region_19.20 | all-reduce | flops 16384 | bytes 65536 | tf_op jit(solution)/shard_map/psum | solution.py:220
  1207.8 35.5 %psum.21 = bf16[1024]{0:T(1024)(128)(2,1)S(1)} all-reduce(bf16[1024]{0:T(1024)(128)(2,1)S(1)} %convert_element_type.153), channel_id=1, replica_groups=mesh['section'=8,'expert'=16,'dp'=2] {'expert'}, use_global_device_ids=true, to_apply=%region_17.18 | all-reduce | flops 1024 | bytes 4096 | tf_op jit(solution)/shard_map/psum | solution.py:219
  (654 shorter events, 628.8 us)
Async XLA Ops:
  13.9 18.6 %all-to-all-start.1 = ((bf16[16,10,1024]{2,1,0:T(8,128)(2,1)}), bf16[16,10,1024]{2,1,0:T(8,128)(2,1)S(1)}, u32[]{:S(2)}, u32[]{:S(2)}) async-start(bf16[16,10,1024]{2,1,0:T(8,128)(2,1)} %reshape.239), calls=%async_computation.1 | async-start | bytes 1048576 | tf_op jit(solution)/shard_map/while/body/eval_jaxpr/all_to_all | solution.py:164
  32.5 14.1 %all-to-all-start = ((bf16[16,10,1024]{2,1,0:T(8,128)(2,1)}), bf16[16,10,1024]{2,1,0:T(8,128)(2,1)S(1)}, u32[]{:S(2)}, u32[]{:S(2)}) async-start(bf16[16,10,1024]{2,1,0:T(8,128)(2,1)} %reshape.238), calls=%async_computation | async-start | bytes 1048576 | tf_op jit(solution)/shard_map/while/body/eval_jaxpr/all_to_all | solution.py:165
  36.1 37.6 %reduce-scatter.3.cloned.1.call-start = ((), (), s32[]{:S(2)}) async-start(), calls=%async_computation.6 | async-start | bytes 24576 | tf_op jit(solution)/shard_map/while/body/eval_jaxpr/reduce_scatter | solution.py:174
  50.0 42.5 %reduce-scatter.5.cloned.1.call-start = ((), (), s32[]{:S(2)}) async-start(), calls=%async_computation.7 | async-start | bytes 3145728 | tf_op jit(solution)/shard_map/while/body/eval_jaxpr/reduce_scatter | solution.py:173
  75.0 14.3 %all-to-all-start.2 = ((bf16[16,1,10]{2,1,0:T(2,128)(2,1)}), bf16[16,1,10]{2,1,0:T(2,128)(2,1)S(1)}, u32[]{:S(2)}, u32[]{:S(2)}) async-start(bf16[16,1,10]{2,1,0:T(2,128)(2,1)} %copy.45), calls=%async_computation.3 | async-start | bytes 16384 | tf_op jit(solution)/shard_map/while/body/eval_jaxpr/all_to_all | solution.py:180
  94.5 18.8 %all-to-all-start.3 = ((bf16[16,10,1024]{2,1,0:T(8,128)(2,1)}), bf16[16,10,1024]{2,1,0:T(8,128)(2,1)S(1)}, u32[]{:S(2)}, u32[]{:S(2)}) async-start(bf16[16,10,1024]{2,1,0:T(8,128)(2,1)} %convert_element_type.283), calls=%async_computation.5 | async-start | bytes 1048576 | tf_op jit(solution)/shard_map/while/body/eval_jaxpr/all_to_all | solution.py:177
  141.8 13.7 %all-to-all-start = ((bf16[16,10,1024]{2,1,0:T(8,128)(2,1)}), bf16[16,10,1024]{2,1,0:T(8,128)(2,1)S(1)}, u32[]{:S(2)}, u32[]{:S(2)}) async-start(bf16[16,10,1024]{2,1,0:T(8,128)(2,1)} %reshape.238), calls=%async_computation | async-start | bytes 1048576 | tf_op jit(solution)/shard_map/while/body/eval_jaxpr/all_to_all | solution.py:165
  145.4 35.4 %reduce-scatter.3.cloned.1.call-start = ((), (), s32[]{:S(2)}) async-start(), calls=%async_computation.6 | async-start | bytes 24576 | tf_op jit(solution)/shard_map/while/body/eval_jaxpr/reduce_scatter | solution.py:174
  158.8 40.5 %reduce-scatter.5.cloned.1.call-start = ((), (), s32[]{:S(2)}) async-start(), calls=%async_computation.7 | async-start | bytes 3145728 | tf_op jit(solution)/shard_map/while/body/eval_jaxpr/reduce_scatter | solution.py:173
  182.1 14.3 %all-to-all-start.2 = ((bf16[16,1,10]{2,1,0:T(2,128)(2,1)}), bf16[16,1,10]{2,1,0:T(2,128)(2,1)S(1)}, u32[]{:S(2)}, u32[]{:S(2)}) async-start(bf16[16,1,10]{2,1,0:T(2,128)(2,1)} %copy.45), calls=%async_computation.3 | async-start | bytes 16384 | tf_op jit(solution)/shard_map/while/body/eval_jaxpr/all_to_all | solution.py:180
  201.5 18.8 %all-to-all-start.3 = ((bf16[16,10,1024]{2,1,0:T(8,128)(2,1)}), bf16[16,10,1024]{2,1,0:T(8,128)(2,1)S(1)}, u32[]{:S(2)}, u32[]{:S(2)}) async-start(bf16[16,10,1024]{2,1,0:T(8,128)(2,1)} %convert_element_type.283), calls=%async_computation.5 | async-start | bytes 1048576 | tf_op jit(solution)/shard_map/while/body/eval_jaxpr/all_to_all | solution.py:177
  248.8 13.7 %all-to-all-start = ((bf16[16,10,1024]{2,1,0:T(8,128)(2,1)}), bf16[16,10,1024]{2,1,0:T(8,128)(2,1)S(1)}, u32[]{:S(2)}, u32[]{:S(2)}) async-start(bf16[16,10,1024]{2,1,0:T(8,128)(2,1)} %reshape.238), calls=%async_computation | async-start | bytes 1048576 | tf_op jit(solution)/shard_map/while/body/eval_jaxpr/all_to_all | solution.py:165
  252.3 36.1 %reduce-scatter.3.cloned.1.call-start = ((), (), s32[]{:S(2)}) async-start(), calls=%async_computation.6 | async-start | bytes 24576 | tf_op jit(solution)/shard_map/while/body/eval_jaxpr/reduce_scatter | solution.py:174
  265.8 41.3 %reduce-scatter.5.cloned.1.call-start = ((), (), s32[]{:S(2)}) async-start(), calls=%async_computation.7 | async-start | bytes 3145728 | tf_op jit(solution)/shard_map/while/body/eval_jaxpr/reduce_scatter | solution.py:173
  289.8 14.3 %all-to-all-start.2 = ((bf16[16,1,10]{2,1,0:T(2,128)(2,1)}), bf16[16,1,10]{2,1,0:T(2,128)(2,1)S(1)}, u32[]{:S(2)}, u32[]{:S(2)}) async-start(bf16[16,1,10]{2,1,0:T(2,128)(2,1)} %copy.45), calls=%async_computation.3 | async-start | bytes 16384 | tf_op jit(solution)/shard_map/while/body/eval_jaxpr/all_to_all | solution.py:180
  309.2 18.8 %all-to-all-start.3 = ((bf16[16,10,1024]{2,1,0:T(8,128)(2,1)}), bf16[16,10,1024]{2,1,0:T(8,128)(2,1)S(1)}, u32[]{:S(2)}, u32[]{:S(2)}) async-start(bf16[16,10,1024]{2,1,0:T(8,128)(2,1)} %convert_element_type.283), calls=%async_computation.5 | async-start | bytes 1048576 | tf_op jit(solution)/shard_map/while/body/eval_jaxpr/all_to_all | solution.py:177
  356.5 13.7 %all-to-all-start = ((bf16[16,10,1024]{2,1,0:T(8,128)(2,1)}), bf16[16,10,1024]{2,1,0:T(8,128)(2,1)S(1)}, u32[]{:S(2)}, u32[]{:S(2)}) async-start(bf16[16,10,1024]{2,1,0:T(8,128)(2,1)} %reshape.238), calls=%async_computation | async-start | bytes 1048576 | tf_op jit(solution)/shard_map/while/body/eval_jaxpr/all_to_all | solution.py:165
  360.1 37.0 %reduce-scatter.3.cloned.1.call-start = ((), (), s32[]{:S(2)}) async-start(), calls=%async_computation.6 | async-start | bytes 24576 | tf_op jit(solution)/shard_map/while/body/eval_jaxpr/reduce_scatter | solution.py:174
  373.5 42.3 %reduce-scatter.5.cloned.1.call-start = ((), (), s32[]{:S(2)}) async-start(), calls=%async_computation.7 | async-start | bytes 3145728 | tf_op jit(solution)/shard_map/while/body/eval_jaxpr/reduce_scatter | solution.py:173
  398.3 14.3 %all-to-all-start.2 = ((bf16[16,1,10]{2,1,0:T(2,128)(2,1)}), bf16[16,1,10]{2,1,0:T(2,128)(2,1)S(1)}, u32[]{:S(2)}, u32[]{:S(2)}) async-start(bf16[16,1,10]{2,1,0:T(2,128)(2,1)} %copy.45), calls=%async_computation.3 | async-start | bytes 16384 | tf_op jit(solution)/shard_map/while/body/eval_jaxpr/all_to_all | solution.py:180
  417.9 18.8 %all-to-all-start.3 = ((bf16[16,10,1024]{2,1,0:T(8,128)(2,1)}), bf16[16,10,1024]{2,1,0:T(8,128)(2,1)S(1)}, u32[]{:S(2)}, u32[]{:S(2)}) async-start(bf16[16,10,1024]{2,1,0:T(8,128)(2,1)} %convert_element_type.283), calls=%async_computation.5 | async-start | bytes 1048576 | tf_op jit(solution)/shard_map/while/body/eval_jaxpr/all_to_all | solution.py:177
  465.2 13.7 %all-to-all-start = ((bf16[16,10,1024]{2,1,0:T(8,128)(2,1)}), bf16[16,10,1024]{2,1,0:T(8,128)(2,1)S(1)}, u32[]{:S(2)}, u32[]{:S(2)}) async-start(bf16[16,10,1024]{2,1,0:T(8,128)(2,1)} %reshape.238), calls=%async_computation | async-start | bytes 1048576 | tf_op jit(solution)/shard_map/while/body/eval_jaxpr/all_to_all | solution.py:165
  468.8 37.0 %reduce-scatter.3.cloned.1.call-start = ((), (), s32[]{:S(2)}) async-start(), calls=%async_computation.6 | async-start | bytes 24576 | tf_op jit(solution)/shard_map/while/body/eval_jaxpr/reduce_scatter | solution.py:174
  496.4 27.9 %reduce-scatter.5.cloned.1.call-start = ((), (), s32[]{:S(2)}) async-start(), calls=%async_computation.7 | async-start | bytes 3145728 | tf_op jit(solution)/shard_map/while/body/eval_jaxpr/reduce_scatter | solution.py:173
  507.0 14.3 %all-to-all-start.2 = ((bf16[16,1,10]{2,1,0:T(2,128)(2,1)}), bf16[16,1,10]{2,1,0:T(2,128)(2,1)S(1)}, u32[]{:S(2)}, u32[]{:S(2)}) async-start(bf16[16,1,10]{2,1,0:T(2,128)(2,1)} %copy.45), calls=%async_computation.3 | async-start | bytes 16384 | tf_op jit(solution)/shard_map/while/body/eval_jaxpr/all_to_all | solution.py:180
  526.4 18.8 %all-to-all-start.3 = ((bf16[16,10,1024]{2,1,0:T(8,128)(2,1)}), bf16[16,10,1024]{2,1,0:T(8,128)(2,1)S(1)}, u32[]{:S(2)}, u32[]{:S(2)}) async-start(bf16[16,10,1024]{2,1,0:T(8,128)(2,1)} %convert_element_type.283), calls=%async_computation.5 | async-start | bytes 1048576 | tf_op jit(solution)/shard_map/while/body/eval_jaxpr/all_to_all | solution.py:177
  577.3 37.0 %reduce-scatter.3.cloned.1.call-start = ((), (), s32[]{:S(2)}) async-start(), calls=%async_computation.6 | async-start | bytes 24576 | tf_op jit(solution)/shard_map/while/body/eval_jaxpr/reduce_scatter | solution.py:174
  605.0 27.9 %reduce-scatter.5.cloned.1.call-start = ((), (), s32[]{:S(2)}) async-start(), calls=%async_computation.7 | async-start | bytes 3145728 | tf_op jit(solution)/shard_map/while/body/eval_jaxpr/reduce_scatter | solution.py:173
  615.6 14.3 %all-to-all-start.2 = ((bf16[16,1,10]{2,1,0:T(2,128)(2,1)}), bf16[16,1,10]{2,1,0:T(2,128)(2,1)S(1)}, u32[]{:S(2)}, u32[]{:S(2)}) async-start(bf16[16,1,10]{2,1,0:T(2,128)(2,1)} %copy.45), calls=%async_computation.3 | async-start | bytes 16384 | tf_op jit(solution)/shard_map/while/body/eval_jaxpr/all_to_all | solution.py:180
  635.0 18.8 %all-to-all-start.3 = ((bf16[16,10,1024]{2,1,0:T(8,128)(2,1)}), bf16[16,10,1024]{2,1,0:T(8,128)(2,1)S(1)}, u32[]{:S(2)}, u32[]{:S(2)}) async-start(bf16[16,10,1024]{2,1,0:T(8,128)(2,1)} %convert_element_type.283), calls=%async_computation.5 | async-start | bytes 1048576 | tf_op jit(solution)/shard_map/while/body/eval_jaxpr/all_to_all | solution.py:177
  682.3 13.7 %all-to-all-start = ((bf16[16,10,1024]{2,1,0:T(8,128)(2,1)}), bf16[16,10,1024]{2,1,0:T(8,128)(2,1)S(1)}, u32[]{:S(2)}, u32[]{:S(2)}) async-start(bf16[16,10,1024]{2,1,0:T(8,128)(2,1)} %reshape.238), calls=%async_computation | async-start | bytes 1048576 | tf_op jit(solution)/shard_map/while/body/eval_jaxpr/all_to_all | solution.py:165
  685.9 36.0 %reduce-scatter.3.cloned.1.call-start = ((), (), s32[]{:S(2)}) async-start(), calls=%async_computation.6 | async-start | bytes 24576 | tf_op jit(solution)/shard_map/while/body/eval_jaxpr/reduce_scatter | solution.py:174
  713.6 26.9 %reduce-scatter.5.cloned.1.call-start = ((), (), s32[]{:S(2)}) async-start(), calls=%async_computation.7 | async-start | bytes 3145728 | tf_op jit(solution)/shard_map/while/body/eval_jaxpr/reduce_scatter | solution.py:173
  723.1 14.3 %all-to-all-start.2 = ((bf16[16,1,10]{2,1,0:T(2,128)(2,1)}), bf16[16,1,10]{2,1,0:T(2,128)(2,1)S(1)}, u32[]{:S(2)}, u32[]{:S(2)}) async-start(bf16[16,1,10]{2,1,0:T(2,128)(2,1)} %copy.45), calls=%async_computation.3 | async-start | bytes 16384 | tf_op jit(solution)/shard_map/while/body/eval_jaxpr/all_to_all | solution.py:180
  742.6 18.8 %all-to-all-start.3 = ((bf16[16,10,1024]{2,1,0:T(8,128)(2,1)}), bf16[16,10,1024]{2,1,0:T(8,128)(2,1)S(1)}, u32[]{:S(2)}, u32[]{:S(2)}) async-start(bf16[16,10,1024]{2,1,0:T(8,128)(2,1)} %convert_element_type.283), calls=%async_computation.5 | async-start | bytes 1048576 | tf_op jit(solution)/shard_map/while/body/eval_jaxpr/all_to_all | solution.py:177
  793.4 33.8 %reduce-scatter.3.cloned.1.call-start = ((), (), s32[]{:S(2)}) async-start(), calls=%async_computation.6 | async-start | bytes 24576 | tf_op jit(solution)/shard_map/while/body/eval_jaxpr/reduce_scatter | solution.py:174
  806.9 38.9 %reduce-scatter.5.cloned.1.call-start = ((), (), s32[]{:S(2)}) async-start(), calls=%async_computation.7 | async-start | bytes 3145728 | tf_op jit(solution)/shard_map/while/body/eval_jaxpr/reduce_scatter | solution.py:173
  828.5 14.3 %all-to-all-start.2 = ((bf16[16,1,10]{2,1,0:T(2,128)(2,1)}), bf16[16,1,10]{2,1,0:T(2,128)(2,1)S(1)}, u32[]{:S(2)}, u32[]{:S(2)}) async-start(bf16[16,1,10]{2,1,0:T(2,128)(2,1)} %copy.45), calls=%async_computation.3 | async-start | bytes 16384 | tf_op jit(solution)/shard_map/while/body/eval_jaxpr/all_to_all | solution.py:180
  847.9 18.8 %all-to-all-start.3 = ((bf16[16,10,1024]{2,1,0:T(8,128)(2,1)}), bf16[16,10,1024]{2,1,0:T(8,128)(2,1)S(1)}, u32[]{:S(2)}, u32[]{:S(2)}) async-start(bf16[16,10,1024]{2,1,0:T(8,128)(2,1)} %convert_element_type.283), calls=%async_computation.5 | async-start | bytes 1048576 | tf_op jit(solution)/shard_map/while/body/eval_jaxpr/all_to_all | solution.py:177
  898.8 32.8 %reduce-scatter.3.cloned.1.call-start = ((), (), s32[]{:S(2)}) async-start(), calls=%async_computation.6 | async-start | bytes 24576 | tf_op jit(solution)/shard_map/while/body/eval_jaxpr/reduce_scatter | solution.py:174
  912.3 37.9 %reduce-scatter.5.cloned.1.call-start = ((), (), s32[]{:S(2)}) async-start(), calls=%async_computation.7 | async-start | bytes 3145728 | tf_op jit(solution)/shard_map/while/body/eval_jaxpr/reduce_scatter | solution.py:173
  932.9 14.3 %all-to-all-start.2 = ((bf16[16,1,10]{2,1,0:T(2,128)(2,1)}), bf16[16,1,10]{2,1,0:T(2,128)(2,1)S(1)}, u32[]{:S(2)}, u32[]{:S(2)}) async-start(bf16[16,1,10]{2,1,0:T(2,128)(2,1)} %copy.45), calls=%async_computation.3 | async-start | bytes 16384 | tf_op jit(solution)/shard_map/while/body/eval_jaxpr/all_to_all | solution.py:180
  952.3 18.8 %all-to-all-start.3 = ((bf16[16,10,1024]{2,1,0:T(8,128)(2,1)}), bf16[16,10,1024]{2,1,0:T(8,128)(2,1)S(1)}, u32[]{:S(2)}, u32[]{:S(2)}) async-start(bf16[16,10,1024]{2,1,0:T(8,128)(2,1)} %convert_element_type.283), calls=%async_computation.5 | async-start | bytes 1048576 | tf_op jit(solution)/shard_map/while/body/eval_jaxpr/all_to_all | solution.py:177
  999.6 13.7 %all-to-all-start = ((bf16[16,10,1024]{2,1,0:T(8,128)(2,1)}), bf16[16,10,1024]{2,1,0:T(8,128)(2,1)S(1)}, u32[]{:S(2)}, u32[]{:S(2)}) async-start(bf16[16,10,1024]{2,1,0:T(8,128)(2,1)} %reshape.238), calls=%async_computation | async-start | bytes 1048576 | tf_op jit(solution)/shard_map/while/body/eval_jaxpr/all_to_all | solution.py:165
  1003.1 31.8 %reduce-scatter.3.cloned.1.call-start = ((), (), s32[]{:S(2)}) async-start(), calls=%async_computation.6 | async-start | bytes 24576 | tf_op jit(solution)/shard_map/while/body/eval_jaxpr/reduce_scatter | solution.py:174
  1016.6 37.0 %reduce-scatter.5.cloned.1.call-start = ((), (), s32[]{:S(2)}) async-start(), calls=%async_computation.7 | async-start | bytes 3145728 | tf_op jit(solution)/shard_map/while/body/eval_jaxpr/reduce_scatter | solution.py:173
  1036.3 14.3 %all-to-all-start.2 = ((bf16[16,1,10]{2,1,0:T(2,128)(2,1)}), bf16[16,1,10]{2,1,0:T(2,128)(2,1)S(1)}, u32[]{:S(2)}, u32[]{:S(2)}) async-start(bf16[16,1,10]{2,1,0:T(2,128)(2,1)} %copy.45), calls=%async_computation.3 | async-start | bytes 16384 | tf_op jit(solution)/shard_map/while/body/eval_jaxpr/all_to_all | solution.py:180
  1055.7 18.8 %all-to-all-start.3 = ((bf16[16,10,1024]{2,1,0:T(8,128)(2,1)}), bf16[16,10,1024]{2,1,0:T(8,128)(2,1)S(1)}, u32[]{:S(2)}, u32[]{:S(2)}) async-start(bf16[16,10,1024]{2,1,0:T(8,128)(2,1)} %convert_element_type.283), calls=%async_computation.5 | async-start | bytes 1048576 | tf_op jit(solution)/shard_map/while/body/eval_jaxpr/all_to_all | solution.py:177
  (69 other events, 586.3 us)
Sparse Core Ops, SparseCore 0:
  50.1 23.5 reduce-scatter.2
  76.1 16.2 reduce-scatter.4
  159.0 21.7 reduce-scatter.2
  183.1 16.2 reduce-scatter.4
  265.9 22.5 reduce-scatter.2
  290.8 16.2 reduce-scatter.4
  373.6 23.3 reduce-scatter.2
  399.5 16.2 reduce-scatter.4
  496.6 9.1 reduce-scatter.2
  508.1 16.2 reduce-scatter.4
  605.1 9.1 reduce-scatter.2
  616.6 16.2 reduce-scatter.4
  713.7 8.1 reduce-scatter.2
  724.2 16.2 reduce-scatter.4
  807.0 20.1 reduce-scatter.2
  829.6 16.2 reduce-scatter.4
  912.4 19.1 reduce-scatter.2
  933.9 16.2 reduce-scatter.4
  1016.7 18.1 reduce-scatter.2
  1037.3 16.2 reduce-scatter.4
